TPU v7x, 512 devices: a whole 4x8x8 slice. The times are simulated.
512 devices in a mesh: dp: 64 (over y_lo, z, core), node: 8 (over x, y_hi).
Axes of the slice: x: 4, y: 8 (y_hi: 2, y_lo: 4; y = y_hi * 4 + y_lo), z: 8, core: 2. Of those that a mesh axis runs over, the one named last changes fastest.
Arguments:
- tokens: bfloat16 [1024, 4096], P('dp', 'node'), may hold values from -200 to 200
- cotangent: bfloat16 [1024, 4096], P('dp', 'node'), may hold values from -6 to 6
- norm_gain: float32 [4096], P('node'), may hold values from 0.1 to 1.9
- gate_weight: bfloat16 [10240, 4096], P('dp', 'node'), may hold values from -0.09375 to 0.09375
- up_weight: bfloat16 [10240, 4096], P('dp', 'node'), may hold values from -0.09375 to 0.09375
- down_weight: bfloat16 [10240, 4096], P('dp', 'node'), may hold values from -0.0625 to 0.0625
Outputs:
- branch_out: bfloat16 [1024, 4096], P('dp', 'node')
- grad_tokens: bfloat16 [1024, 4096], P('dp', 'node')
- grad_gate_weight: float32 [10240, 4096], P('dp', 'node')
- grad_up_weight: float32 [10240, 4096], P('dp', 'node')
- grad_down_weight: float32 [10240, 4096], P('dp', 'node')
- grad_norm_gain: float32 [4096], P('node')
All inputs are finite; a program needn't handle non-finite values.
Results may differ from a plain program's by a relative error of at most 0.0065.
Values may be sent and summed in bfloat16 or wider, within the bound.
A program may use at most 64 MiB of HBM per device.

v0:
```python
import math

import jax
import jax.numpy as jnp
from jax import lax
from jax.sharding import PartitionSpec as P

D = 4096


EPSILON = 1e-06
GELU_SCALE = math.sqrt(2.0 / math.pi)


def gelu_parts(value):
    inner = GELU_SCALE * (value + 0.044715 * value * value * value)
    tanh_inner = jnp.tanh(inner)
    activated = 0.5 * value * (1.0 + tanh_inner)
    slope = 0.5 * (1.0 + tanh_inner) + 0.5 * value * (
        1.0 - tanh_inner * tanh_inner
    ) * GELU_SCALE * (1.0 + 3.0 * 0.044715 * value * value)
    return (activated, slope)


def activation_grads(back_sum, up_value, activated, slope):
    return jnp.stack([back_sum * up_value * slope, back_sum * activated]).astype(jnp.bfloat16)


def on_device(tokens, cotangent, norm_gain, gate_weight, up_weight, down_weight):
    widened = tokens.astype(jnp.float32)
    square_part = jnp.sum(widened * widened, axis=1)
    mean_square = lax.psum(square_part, "node") / D
    inv_rms = lax.rsqrt(mean_square + EPSILON)
    scaled = widened * inv_rms[:, None]
    normed = (scaled * norm_gain).astype(jnp.bfloat16)
    normed_all = lax.all_gather(normed, "dp", axis=0, tiled=True)
    both_weights = jnp.stack([gate_weight, up_weight])
    partials = lax.dot_general(
        both_weights, normed_all, (((2,), (1,)), ((), ())), preferred_element_type=jnp.float32
    )
    summed = lax.psum(partials, "node")
    gate_value, up_value = (summed[0], summed[1])
    activated, slope = gelu_parts(gate_value)
    hidden = (activated * up_value).astype(jnp.bfloat16)
    columns = hidden
    branch_out = lax.psum_scatter(
        lax.dot_general(
            columns, down_weight, (((0,), (0,)), ((), ())), preferred_element_type=jnp.float32
        ),
        "dp",
        scatter_dimension=0,
        tiled=True,
    ).astype(jnp.bfloat16)
    cot_all = lax.all_gather(cotangent, "dp", axis=0, tiled=True)
    back_part = lax.dot_general(
        down_weight, cot_all, (((1,), (1,)), ((), ())), preferred_element_type=jnp.float32
    )
    grad_down_weight = lax.dot_general(
        hidden, cot_all, (((1,), (0,)), ((), ())), preferred_element_type=jnp.float32
    )
    back_sum = lax.psum(back_part, "node")
    grad_pair = activation_grads(back_sum, up_value, activated, slope)
    weight_grads = lax.dot_general(
        grad_pair, normed_all, (((2,), (0,)), ((), ())), preferred_element_type=jnp.float32
    )
    columns = grad_pair
    grad_normed = lax.psum_scatter(
        lax.dot_general(
            columns, both_weights, (((0, 1), (0, 1)), ((), ())), preferred_element_type=jnp.float32
        ),
        "dp",
        scatter_dimension=0,
        tiled=True,
    )
    grad_scaled = grad_normed * norm_gain
    row_part = jnp.sum(grad_scaled * scaled, axis=1)
    gain_part = jnp.sum(grad_normed * scaled, axis=0)
    row_total = lax.psum(row_part, "node")
    gain_total = lax.psum(gain_part, "dp")
    grad_tokens = (inv_rms[:, None] * (grad_scaled - scaled * (row_total / D)[:, None])).astype(
        jnp.bfloat16
    )
    return (branch_out, grad_tokens, weight_grads[0], weight_grads[1], grad_down_weight, gain_total)


def solution(mesh):
    in_specs = (
        P("dp", "node"),
        P("dp", "node"),
        P("node"),
        P("dp", "node"),
        P("dp", "node"),
        P("dp", "node"),
    )
    out_specs = (
        P("dp", "node"),
        P("dp", "node"),
        P("dp", "node"),
        P("dp", "node"),
        P("dp", "node"),
        P("node"),
    )
    return jax.shard_map(
        on_device, mesh=mesh, in_specs=in_specs, out_specs=out_specs, check_vma=False
    )
```

profile of v0, /device:TPU:1, one launch (start us, length us, event | category | flops | bytes accessed | tf_op | source)
XLA Modules:
  0.0 1009.6 jit_solution(3409829580218216988)
XLA Ops:
  7.2 0.0 copy-start
  7.2 0.0 all-gather.5.cloned.1.call-start
  7.2 0.7 all-gather.5.cloned.1.call-update
  7.9 0.0 all-gather.3.cloned.1.call-start
  8.0 0.8 fusion.23
  8.8 28.9 %psum.35 = f32[16]{0:T(128)S(1)} all-reduce(f32[16]{0:T(128)S(1)} %fusion.23), channel_id=1, replica_groups=mesh['dp'=64,'node'=8] {'node'}, use_global_device_ids=true, to_apply=%region_1.0 | all-reduce | flops 16 | bytes 128 | tf_op jit(solution)/shard_map/psum | solution.py:32
  37.7 1.4 fusion.17
  39.1 0.0 all-gather.3.cloned.1.call-update
  39.2 0.0 all-reduce.3.cloned.1.call-start
  39.2 92.5 %all-gather.5.cloned.1.call-done = bf16[1024,512]{1,0:T(8,128)(2,1)} async-done(((bf16[16,512]{1,0:T(8,128)(2,1)}), bf16[1024,512]{1,0:T(8,128)(2,1)}) %all-gather.5.cloned.1.call-update) | async-done | bytes 1048592 | tf_op jit(solution)/shard_map/all_gather | solution.py:54
  131.7 0.0 copy-done
  131.7 2.6 fusion.28
  134.3 114.8 %all-gather.3.cloned.1.call-done = bf16[1024,512]{1,0:T(8,128)(2,1)} async-done(((bf16[16,512]{1,0:T(8,128)(2,1)}), bf16[1024,512]{1,0:T(8,128)(2,1)}) %all-gather.3.cloned.1.call-update) | async-done | bytes 1048592 | tf_op jit(solution)/shard_map/all_gather | solution.py:36
  249.1 3.0 fusion.2
  252.1 0.0 copy-start.4
  252.1 0.0 copy-start.5
  252.1 0.0 all-reduce.3.cloned.1.call-update
  252.2 0.0 reduce-scatter.5.cloned.1.call-start
  252.2 190.3 %all-reduce.3.cloned.1.call-done = (f32[2,160,1024]{2,1,0:T(8,128)}, f32[160,1024]{1,0:T(8,128)}) async-done(((f32[2,160,1024]{2,1,0:T(8,128)}, f32[160,1024]{1,0:T(8,128)}), (f32[2,160,1024]{2,1,0:T(8,128)}, f32[160,1024]{1,0:T(8,128)})) %all-reduce.3.cloned.1.call-update) | async-done | bytes 1966096 | tf_op jit(solution)/shard_map/psum | solution.py:41
  442.5 2.0 fusion.12
  444.5 0.0 copy-done.4
  444.6 0.0 copy-done.5
  444.6 2.1 convolution_bitcast_fusion
  446.6 0.0 reduce-scatter.5.cloned.1.call-update
  446.6 0.0 reduce-scatter.3.cloned.1.call-start
  446.7 0.0 copy-start.2
  446.7 1.8 fusion.27
  448.5 0.0 reduce-scatter.3.cloned.1.call-update
  448.6 0.0 copy-done.2
  448.6 0.0 copy-start.1
  448.6 0.5 fusion
  449.1 0.0 copy-start.3
  449.1 0.0 copy-start.6
  449.1 0.9 slice_bitcast_fusion.2
  450.0 0.0 copy-done.1
  450.0 1.1 fusion.29
  451.0 271.4 %reduce-scatter.5.cloned.1.call-done = f32[16,512]{1,0:T(8,128)} async-done(((f32[1024,512]{1,0:T(8,128)}), f32[16,512]{1,0:T(8,128)}) %reduce-scatter.5.cloned.1.call-update) | async-done | bytes 32784 | tf_op jit(solution)/shard_map/reduce_scatter | solution.py:67
  722.4 0.0 copy-done.3
  722.4 0.0 copy-done.6
  722.4 1.0 fusion.22
  723.4 26.7 %psum.38 = f32[16]{0:T(128)S(1)} all-reduce(f32[16]{0:T(128)S(1)} %get-tuple-element.7), channel_id=1, replica_groups=mesh['dp'=64,'node'=8] {'node'}, use_global_device_ids=true, to_apply=%region_7.0 | all-reduce | flops 16 | bytes 128 | tf_op jit(solution)/shard_map/psum | solution.py:78
  750.1 141.8 %psum.39 = f32[512]{0:T(512)} all-reduce(f32[512]{0:T(512)S(1)} %get-tuple-element.6), channel_id=1, replica_groups=mesh['dp'=64,'node'=8] {'dp'}, use_global_device_ids=true, to_apply=%region_9.0 | all-reduce | flops 512 | bytes 4096 | tf_op jit(solution)/shard_map/psum | solution.py:79
  891.9 1.4 fusion.21
  893.3 108.4 %reduce-scatter.3.cloned.1.call-done = f32[16,512]{1,0:T(8,128)} async-done(((f32[1024,512]{1,0:T(8,128)}), f32[16,512]{1,0:T(8,128)}) %reduce-scatter.3.cloned.1.call-update) | async-done | bytes 32784 | tf_op jit(solution)/shard_map/reduce_scatter | solution.py:46
  1001.7 1.4 convert_element_type.19
  (2 shorter events, 0.0 us)
Async XLA Ops:
  7.2 124.6 %copy-start = (bf16[160,512]{1,0:T(8,128)(2,1)S(1)}, bf16[160,512]{1,0:T(8,128)(2,1)}, u32[]{:S(2)}) copy-start(bf16[160,512]{1,0:T(8,128)(2,1)} %param.11) | copy-start | bytes 491524
  7.2 124.6 %all-gather.5.cloned.1.call-start = ((), (), s32[]{:S(2)}) async-start(), calls=%async_computation.4 | async-start | bytes 1064960 | tf_op jit(solution)/shard_map/all_gather | solution.py:54
  7.9 241.2 %all-gather.3.cloned.1.call-start = ((), (), s32[]{:S(2)}) async-start(), calls=%async_computation.2 | async-start | bytes 1064960 | tf_op jit(solution)/shard_map/all_gather | solution.py:36
  39.2 403.4 %all-reduce.3.cloned.1.call-start = ((), (), s32[]{:S(2)}) async-start(), calls=%async_computation.6 | async-start | bytes 3932160 | tf_op jit(solution)/shard_map/psum | solution.py:41
  252.1 192.4 %copy-start.4 = (bf16[160,512]{1,0:T(8,128)(2,1)S(1)}, bf16[160,512]{1,0:T(8,128)(2,1)}, u32[]{:S(2)}) copy-start(bf16[160,512]{1,0:T(8,128)(2,1)} %param.10) | copy-start | bytes 491524
  252.1 192.4 %copy-start.5 = (bf16[160,512]{1,0:T(8,128)(2,1)S(1)}, bf16[160,512]{1,0:T(8,128)(2,1)}, u32[]{:S(2)}) copy-start(bf16[160,512]{1,0:T(8,128)(2,1)} %param.9) | copy-start | bytes 491524
  252.2 470.3 %reduce-scatter.5.cloned.1.call-start = ((), (), s32[]{:S(2)}) async-start(), calls=%async_computation.5 | async-start | bytes 2129920 | tf_op jit(solution)/shard_map/reduce_scatter | solution.py:67
  446.6 555.1 %reduce-scatter.3.cloned.1.call-start = ((), (), s32[]{:S(2)}) async-start(), calls=%async_computation.3 | async-start | bytes 2129920 | tf_op jit(solution)/shard_map/reduce_scatter | solution.py:46
  446.7 1.9 copy-start.2
  448.6 1.4 copy-start.1
  449.1 273.3 %copy-start.3 = (bf16[16,512]{1,0:T(8,128)(2,1)S(1)}, bf16[16,512]{1,0:T(8,128)(2,1)}, u32[]{:S(2)}) copy-start(bf16[16,512]{1,0:T(8,128)(2,1)} %param.6) | copy-start | bytes 49156
  449.1 273.3 %copy-start.6 = (f32[512]{0:T(512)S(1)}, f32[512]{0:T(512)}, u32[]{:S(2)}) copy-start(f32[512]{0:T(512)} %param.8) | copy-start | bytes 6148
Sparse Core Ops, SparseCore 0:
  10.2 121.5 all-gather.4
  134.5 114.5 all-gather.2
  252.3 190.2 all-reduce.2
  446.8 275.5 reduce-scatter.4
  725.0 276.6 reduce-scatter.2
where the time goes:
time: 1020 us; the launch traced here: 1010 us
  waiting for transfers between devices  778 us (76%)
  blocking collectives  197 us (19%)
  between operations  13.9 us (1%)
  matrix products  11 us (1%)
    reduce_scatter x1, waiting for transfers between devices, on_device(): lax.psum_scatter(lax.dot_general(columns, both_weights, (((0, 1), (0, 1))...  271 us
    psum x1, waiting for transfers between devices, on_device(): summed = lax.psum(partials, 'node')  190 us
    psum x1, blocking collectives, on_device(): gain_total = lax.psum(gain_part, 'dp')  142 us
    all_gather x1, waiting for transfers between devices, on_device(): normed_all = lax.all_gather(normed, 'dp', axis=0, tiled=True)  115 us
    reduce_scatter x1, waiting for transfers between devices, on_device(): lax.psum_scatter(lax.dot_general(columns, down_weight, (((0,), (0,)), (()...  108 us
    all_gather x1, waiting for transfers between devices, on_device(): cot_all = lax.all_gather(cotangent, 'dp', axis=0, tiled=True)  92.5 us
    psum x1, blocking collectives, on_device(): mean_square = lax.psum(square_part, 'node') / D  28.9 us
    psum x1, blocking collectives, on_device(): row_total = lax.psum(row_part, 'node')  26.7 us
  transfers between devices with their start and end apart: 5, of which 5 were waited for; matrix products, arithmetic and copies ran while one was open for 1% of the time, Pallas kernels for 0%

commit v1 on v0

v1 whole, which is shorter than its diff:
```python
import functools
import math

import jax
import jax.numpy as jnp
from jax import lax
from jax.experimental import pallas as pl
from jax.experimental.pallas import tpu as pltpu
from jax.sharding import PartitionSpec as P

D = 4096
EPSILON = 1e-06
GELU_SCALE = math.sqrt(2.0 / math.pi)
MESH = pl.DeviceIdType.MESH
F32 = jnp.float32
BF16 = jnp.bfloat16

GROUPS = ((0, 1), (1, 3), (3, 5), (5, 7), (7, 8))
UNITS = 160
NT = (((1,), (1,)), ((), ()))
TN = (((0,), (0,)), ((), ()))


def dot(a, b, dims=None):
    if dims is None:
        return jnp.dot(a, b, preferred_element_type=F32)
    return lax.dot_general(a, b, dims, preferred_element_type=F32)


def gelu_parts(value):
    inner = GELU_SCALE * (value + 0.044715 * value * value * value)
    tanh_inner = jnp.tanh(inner)
    activated = 0.5 * value * (1.0 + tanh_inner)
    slope = 0.5 * (1.0 + tanh_inner) + 0.5 * value * (
        1.0 - tanh_inner * tanh_inner
    ) * GELU_SCALE * (1.0 + 3.0 * 0.044715 * value * value)
    return (activated, slope)


def pair(value):
    high = value.astype(BF16).astype(F32)
    return high, (value - high).astype(BF16).astype(F32)


def put(wide, lane, *values):
    at = lax.broadcasted_iota(jnp.int32, wide.shape, 1)
    for i, value in enumerate(values):
        wide = jnp.where(at == lane + i, value, wide)
    return wide


class Copies:
    def __init__(self, send_sem, recv_sem):
        self.send_sem, self.recv_sem, self.count, self.all = send_sem, recv_sem, 0, []

    def __call__(self, src, dst, device):
        i = self.count
        self.count += 1
        copy = pltpu.make_async_remote_copy(
            src_ref=src,
            dst_ref=dst,
            send_sem=self.send_sem.at[i],
            recv_sem=self.recv_sem.at[i],
            device_id=device,
            device_id_type=MESH,
        )
        copy.start()
        self.all.append(copy)
        return copy


N_COPIES = 120


def kernel(
    tok_hbm, cot_hbm, gain_hbm, gate_hbm, up_hbm, down_hbm,
    branch_hbm, gtok_hbm, dgate_hbm, dup_hbm, ddown_hbm, dgain_hbm,
    own_tok, gain_v, tok, cot, w, w_high, w_low, wd, part, part_own, rx, y_out, y_in, hid,
    normed, branch_part, gn_part, ring_b, ring_g, ring_b_out, ring_g_out,
    last_b, last_g, last_b_out, last_g_out, last_b_in, last_g_in,
    dw, dd, dw_in, dgain, dgain_in, dgain_y, dgain_y_in, dgain_c, dgain_c_in,
    o_branch, o_gtok, o_dgain,
    send_sem, recv_sem, local_sem,
):
    dp, node = lax.axis_index("dp"), lax.axis_index("node")
    x, yh = node // 2, node % 2
    yl, z, c = dp // 16, (dp // 2) % 8, dp % 2

    def at(dx=0, dyh=0, dyl=0, dz=0, dc=0):
        return (
            lax.rem(yl + dyl, 4) * 16 + lax.rem(z + dz, 8) * 2 + lax.rem(c + dc, 2),
            lax.rem(x + dx, 4) * 2 + lax.rem(yh + dyh, 2),
        )

    sibling, across = at(dc=1), at(dyh=1)
    ahead, behind = at(dz=1), at(dz=7)

    def piece(k):
        return lax.rem(k - x + 8, 4)

    local = []

    def bring(src, dst):
        copy = pltpu.make_async_copy(src, dst, local_sem.at[len(local)])
        copy.start()
        local.append(copy)
        return copy

    mine = piece(0)
    b_tok = bring(tok_hbm, tok.at[0, mine])
    b_cot = bring(cot_hbm, cot.at[0, mine])
    b_own = bring(tok_hbm, own_tok)
    b_gain = bring(gain_hbm, gain_v)
    b_gate = bring(gate_hbm, w.at[pl.ds(0, UNITS)])
    b_up = bring(up_hbm, w.at[pl.ds(2 * UNITS, UNITS)])
    b_down = bring(down_hbm, wd.at[pl.ds(0, UNITS)])

    barrier = pltpu.get_barrier_semaphore()
    partners = [sibling, across]
    partners += [at(dx=k) for k in (1, 2, 3)]
    partners += [at(dyl=k) for k in (1, 2, 3)]
    partners += [at(dz=k) for k in range(1, 8)]
    for device in partners:
        pl.semaphore_signal(barrier, 1, device_id=device, device_id_type=MESH)
    wd[pl.ds(2 * UNITS, 64)] = jnp.zeros((64, 512), BF16)
    pl.semaphore_wait(barrier, len(partners))

    remote = Copies(send_sem, recv_sem)

    y_tok = [remote(tok_hbm, tok.at[0, piece(4 - k)], at(dyl=k)) for k in (1, 2, 3)]
    y_cot = [remote(cot_hbm, cot.at[0, piece(4 - k)], at(dyl=k)) for k in (1, 2, 3)]
    s_gate = remote(gate_hbm, w.at[pl.ds(UNITS, UNITS)], sibling)
    s_up = remote(up_hbm, w.at[pl.ds(3 * UNITS, UNITS)], sibling)
    s_down = remote(down_hbm, wd.at[pl.ds(UNITS, UNITS)], sibling)

    def fold(block):
        rows = pl.ds(block * UNITS, UNITS)
        high, low = pair(w[rows].astype(F32) * gain_v[...])
        w_high[rows] = high.astype(BF16)
        w_low[rows] = low.astype(BF16)

    b_gain.wait()
    b_gate.wait()
    fold(0)
    b_up.wait()
    fold(2)
    b_tok.wait()
    b_cot.wait()
    b_down.wait()
    b_own.wait()

    def ring(buffer, step, both, way):
        copies = []
        if both or way > 0:
            src = 0 if step == 1 else 2 * (step - 1)
            copies.append(remote(buffer.at[src], buffer.at[min(2 * step, 7)], ahead))
        if both or way < 0:
            src = 0 if step == 1 else 2 * (step - 1) - 1
            copies.append(remote(buffer.at[src], buffer.at[2 * step - 1], behind))
        return copies

    for copy in y_tok:
        copy.wait_recv()
    r_tok = ring(tok, 1, True, 0)
    for copy in y_cot:
        copy.wait_recv()
    r_cot = ring(cot, 1, True, 0)

    s_gate.wait_recv()
    fold(1)
    s_up.wait_recv()
    fold(3)
    s_down.wait_recv()

    def multiply(g):
        a, b = GROUPS[g]
        n = b - a
        t = tok[a:b].reshape(n * 64, 512)
        gate_up = dot(t, w_high[...], NT) + dot(t, w_low[...], NT)
        back = dot(cot[a:b].reshape(n * 64, 512), wd[...], NT)
        wide = t.astype(F32)
        back = put(back, 2 * UNITS, *pair(jnp.sum(wide * wide, axis=1, keepdims=True)))
        gate_up = gate_up.reshape(n, 4, 16, 4 * UNITS)
        back = back.reshape(n, 4, 16, 384)
        part[a:b, :, :, 0:640] = gate_up.astype(BF16)
        part[a:b, :, :, 640:1024] = back.astype(BF16)
        part_own[a:b, :, 0:640] = gate_up[:, 0]
        part_own[a:b, :, 640:1024] = back[:, 0]
        return [
            remote(part.at[pl.ds(a, n), k], rx.at[k - 1, pl.ds(a, n)], at(dx=k))
            for k in (1, 2, 3)
        ]

    def add_x(g, copies):
        a, b = GROUPS[g]
        n = b - a
        for copy in copies:
            copy.wait_recv()
        total = part_own[a:b]
        for k in range(3):
            total = total + rx[k, a:b].astype(F32)
        part_own[a:b] = total
        total = total.reshape(n * 16, 1024)
        squares = total[:, 960:961] + total[:, 961:962]
        y_out[a:b, :, 0:640] = total[:, 0:640].astype(BF16).reshape(n, 16, 640)
        last = put(total[:, 640:1024], 320, *pair(squares))
        y_out[a:b, :, 640:1024] = last.astype(BF16).reshape(n, 16, 384)
        return remote(y_out.at[pl.ds(a, n)], y_in.at[pl.ds(a, n)], across)

    x_sent, y_sent = [], []
    x_sent.append(multiply(0))
    for step in (1, 2, 3, 4):
        for copy in r_tok:
            copy.wait_recv()
        if step < 4:
            r_tok = ring(tok, step + 1, step < 3, -1)
        for copy in r_cot:
            copy.wait_recv()
        if step < 4:
            r_cot = ring(cot, step + 1, step < 3, 1)
        x_sent.append(multiply(step))
        y_sent.append(add_x(step - 1, x_sent[step - 1]))
    y_sent.append(add_x(4, x_sent[4]))

    def pointwise(g):
        a, b = GROUPS[g]
        n = b - a
        y_sent[g].wait_recv()
        total = (part_own[a:b] + y_in[a:b].astype(F32)).reshape(n * 16, 1024)
        squares = total[:, 960:961] + total[:, 961:962]
        inv_rms = lax.rsqrt(squares / D + EPSILON)
        gate_value = total[:, 0:320] * inv_rms
        up_value = total[:, 320:640] * inv_rms
        last = total[:, 640:1024]
        back = last[:, 0:320]
        activated, slope = gelu_parts(gate_value)
        grad_gate = (back * up_value * slope).astype(BF16)
        grad_up = (back * activated).astype(BF16)
        along = jnp.sum(
            grad_gate.astype(F32) * gate_value + grad_up.astype(F32) * up_value,
            axis=1,
            keepdims=True,
        )
        hid[a:b, 0, :, 0:640] = jnp.concatenate([grad_gate, grad_up], axis=1).reshape(n, 16, 640)
        hidden = jnp.concatenate([activated * up_value, jnp.zeros((n * 16, 64), F32)], axis=1)
        hidden = put(hidden, 320, *pair(along), *pair(inv_rms))
        hid[a:b, 0, :, 640:1024] = hidden.astype(BF16).reshape(n, 16, 384)
        return [
            remote(hid.at[pl.ds(a, n), 0], hid.at[pl.ds(a, n), 4 - k], at(dx=k))
            for k in (1, 2, 3)
        ]

    h_sent = {g: pointwise(g) for g in (0, 1, 4, 3, 2)}

    def inverse(block):
        return block[:, 962:963].astype(F32) + block[:, 963:964].astype(F32)

    def terms(g, gain_sum):
        a, b = GROUPS[g]
        n = b - a
        for copy in h_sent[g]:
            copy.wait_recv()
        block = hid[a:b].reshape(n * 64, 1024)
        branch_part[a:b] = dot(block[:, 640:1024], wd[...]).reshape(n, 64, 512)
        grad = dot(block[:, 0:640], w[...])
        scaled = tok[a:b].reshape(n * 64, 512).astype(F32) * inverse(block)
        normed[a:b] = (scaled * gain_v[...]).astype(BF16).reshape(n, 64, 512)
        gain_sum = gain_sum + jnp.sum(grad * scaled, axis=0, keepdims=True)
        gn_part[a:b, :, 0:512] = grad.reshape(n, 64, 512)
        along = block[:, 960:961].astype(F32) + block[:, 961:962].astype(F32)
        extra = put(jnp.zeros((n * 64, 128), F32), 0, along)
        gn_part[a:b, :, 512:640] = extra.reshape(n, 64, 128)
        return gain_sum

    def rounded(total):
        along = total[:, 512:513] + total[:, 513:514]
        return jnp.concatenate(
            [total[:, 0:512].astype(BF16), put(total[:, 512:640], 0, *pair(along)).astype(BF16)],
            axis=1,
        )

    gain_sum = jnp.zeros((1, 512), F32)
    gain_sum = terms(4, gain_sum)
    ring_b_out[0, 0] = branch_part[7].astype(BF16)
    ring_g_out[0, 1] = rounded(gn_part[7])
    arrived_b = {0: remote(ring_b_out.at[0, 0], ring_b.at[0, 0], ahead)}
    arrived_g = {1: remote(ring_g_out.at[0, 1], ring_g.at[0, 1], behind)}
    for step in (2, 3, 4):
        distance = 5 - step
        gain_sum = terms(distance, gain_sum)
        next_b, next_g = {}, {}
        for way in (0, 1):
            slot = 2 * distance - 1 + way
            there = (ahead, behind)[way]
            total = branch_part[slot]
            if way in arrived_b:
                arrived_b[way].wait_recv()
                total = total + ring_b[step - 2, way].astype(F32)
            ring_b_out[step - 1, way] = total.astype(BF16)
            next_b[way] = remote(ring_b_out.at[step - 1, way], ring_b.at[step - 1, way], there)
        for way in (0, 1):
            slot = 2 * distance - 1 + way
            there = (ahead, behind)[way]
            total = gn_part[slot]
            if way in arrived_g:
                arrived_g[way].wait_recv()
                total = total + ring_g[step - 2, way].astype(F32)
            ring_g_out[step - 1, way] = rounded(total)
            next_g[way] = remote(ring_g_out.at[step - 1, way], ring_g.at[step - 1, way], there)
        arrived_b, arrived_g = next_b, next_g

    gain_sum = terms(0, gain_sum)
    dgain[...] = jnp.broadcast_to(gain_sum, (8, 512))
    z_gain = [remote(dgain, dgain_in.at[k - 1], at(dz=k)) for k in range(1, 8)]

    every = hid[...].reshape(512, 1024)
    dw[...] = dot(every[:, 0:640], normed[...].reshape(512, 512), TN)
    dd[...] = dot(every[:, 640:1024], cot[...].reshape(512, 512), TN)
    w_sent = [
        remote(dw.at[pl.ds(UNITS, UNITS)], dw_in.at[0], sibling),
        remote(dw.at[pl.ds(3 * UNITS, UNITS)], dw_in.at[1], sibling),
        remote(dd.at[pl.ds(UNITS, UNITS)], dw_in.at[2], sibling),
    ]

    for copy in arrived_b.values():
        copy.wait_recv()
    total = branch_part[0] + ring_b[3, 0].astype(F32) + ring_b[3, 1].astype(F32)
    last_b[...] = total.reshape(4, 16, 512)
    last_b_out[...] = total.astype(BF16).reshape(4, 16, 512)
    y_b = [remote(last_b_out.at[piece(k)], last_b_in.at[k - 1], at(dyl=k)) for k in (1, 2, 3)]
    for copy in arrived_g.values():
        copy.wait_recv()
    total = gn_part[0] + ring_g[3, 0].astype(F32) + ring_g[3, 1].astype(F32)
    last_g[...] = total.reshape(4, 16, 640)
    last_g_out[...] = rounded(total).reshape(4, 16, 640)
    y_g = [remote(last_g_out.at[piece(k)], last_g_in.at[k - 1], at(dyl=k)) for k in (1, 2, 3)]

    for copy in z_gain:
        copy.wait_recv()
    total = dgain[...]
    for k in range(7):
        total = total + dgain_in[k]
    dgain_y[...] = total
    g_y = [remote(dgain_y, dgain_y_in.at[k - 1], at(dyl=k)) for k in (1, 2, 3)]

    for i, (grad, row, out) in enumerate(((dw, 0, dgate_hbm), (dw, 2 * UNITS, dup_hbm), (dd, 0, ddown_hbm))):
        w_sent[i].wait_recv()
        rows = pl.ds(row, UNITS)
        grad[rows] = grad[rows] + dw_in[i]
        bring(grad.at[rows], out)

    for copy in y_b:
        copy.wait_recv()
    total = last_b[mine]
    for k in range(3):
        total = total + last_b_in[k].astype(F32)
    o_branch[...] = total.astype(BF16)
    bring(o_branch, branch_hbm)

    for copy in g_y:
        copy.wait_recv()
    total = dgain_y[...]
    for k in range(3):
        total = total + dgain_y_in[k]
    dgain_c[...] = total
    g_c = remote(dgain_c, dgain_c_in, sibling)

    for copy in y_g:
        copy.wait_recv()
    total = last_g[mine]
    for k in range(3):
        total = total + last_g_in[k].astype(F32)
    row_mean = (total[:, 512:513] + total[:, 513:514]) / D
    inv_rms = inverse(hid[0, mine])
    scaled = own_tok[...].astype(F32) * inv_rms
    o_gtok[...] = (inv_rms * (total[:, 0:512] * gain_v[...] - scaled * row_mean)).astype(BF16)
    bring(o_gtok, gtok_hbm)

    g_c.wait_recv()
    o_dgain[...] = (dgain_c[...] + dgain_c_in[...])[0:1]
    bring(o_dgain, dgain_hbm)

    for copy in remote.all:
        copy.wait_send()
    for copy in local[7:]:
        copy.wait()


def on_device(tokens, cotangent, norm_gain, gate_weight, up_weight, down_weight):
    vmem, dma = pltpu.VMEM, pltpu.SemaphoreType.DMA
    grad = jax.ShapeDtypeStruct((UNITS, 512), F32)
    outs = pl.pallas_call(
        kernel,
        out_shape=(
            jax.ShapeDtypeStruct((16, 512), BF16),
            jax.ShapeDtypeStruct((16, 512), BF16),
            grad,
            grad,
            grad,
            jax.ShapeDtypeStruct((1, 512), F32),
        ),
        in_specs=[pl.BlockSpec(memory_space=pl.ANY)] * 6,
        out_specs=[pl.BlockSpec(memory_space=pl.ANY)] * 6,
        scratch_shapes=[
            vmem((16, 512), BF16),
            vmem((1, 512), F32),
            vmem((8, 4, 16, 512), BF16),
            vmem((8, 4, 16, 512), BF16),
            vmem((4 * UNITS, 512), BF16),
            vmem((4 * UNITS, 512), BF16),
            vmem((4 * UNITS, 512), BF16),
            vmem((384, 512), BF16),
            vmem((8, 4, 16, 1024), BF16),
            vmem((8, 16, 1024), F32),
            vmem((3, 8, 16, 1024), BF16),
            vmem((8, 16, 1024), BF16),
            vmem((8, 16, 1024), BF16),
            vmem((8, 4, 16, 1024), BF16),
            vmem((8, 64, 512), BF16),
            vmem((8, 64, 512), F32),
            vmem((8, 64, 640), F32),
            vmem((4, 2, 64, 512), BF16),
            vmem((4, 2, 64, 640), BF16),
            vmem((4, 2, 64, 512), BF16),
            vmem((4, 2, 64, 640), BF16),
            vmem((4, 16, 512), F32),
            vmem((4, 16, 640), F32),
            vmem((4, 16, 512), BF16),
            vmem((4, 16, 640), BF16),
            vmem((3, 16, 512), BF16),
            vmem((3, 16, 640), BF16),
            vmem((4 * UNITS, 512), F32),
            vmem((384, 512), F32),
            vmem((3, UNITS, 512), F32),
            vmem((8, 512), F32),
            vmem((7, 8, 512), F32),
            vmem((8, 512), F32),
            vmem((3, 8, 512), F32),
            vmem((8, 512), F32),
            vmem((8, 512), F32),
            vmem((16, 512), BF16),
            vmem((16, 512), BF16),
            vmem((1, 512), F32),
            dma((N_COPIES,)),
            dma((N_COPIES,)),
            dma((16,)),
        ],
        compiler_params=pltpu.CompilerParams(
            collective_id=0, has_side_effects=True, vmem_limit_bytes=48 * 1024 * 1024
        ),
        cost_estimate=pl.CostEstimate(flops=1_600_000_000, bytes_accessed=1_600_000, transcendentals=50_000),
    )(tokens, cotangent, norm_gain.reshape(1, 512), gate_weight, up_weight, down_weight)
    return (*outs[:5], outs[5].reshape(512))


def solution(mesh):
    split = P("dp", "node")
    return jax.shard_map(
        on_device,
        mesh=mesh,
        in_specs=(split, split, P("node"), split, split, split),
        out_specs=(split, split, split, split, split, P("node")),
        check_vma=False,
    )
```

time: 1020 us -> 89.7 us (0.09)
  waiting for transfers between devices: 778 us -> 0 us
  blocking collectives: 197 us -> 0 us
  Pallas kernels: 0 us -> 79.9 us
  between operations: 13.9 us -> 0.66 us
  matrix products: 11 us -> 0 us
    reduce_scatter x2 -> x0, waiting for transfers between devices: 380 us -> none  [the longest x1 271 us: on_device(): lax.psum_scatter(lax.dot_general(columns, both_weights, (((0, 1), (0, 1))...]
    all_gather x2 -> x0, waiting for transfers between devices: 207 us -> none  [the longest x1 115 us: on_device(): normed_all = lax.all_gather(normed, 'dp', axis=0, tiled=True)]
    psum x3 -> x0, blocking collectives: 197 us -> none  [the longest x1 142 us: on_device(): gain_total = lax.psum(gain_part, 'dp')]
    psum x1 -> x0, waiting for transfers between devices: 190 us -> none  [on_device(): summed = lax.psum(partials, 'node')]
    pallas_call x0 -> x1, Pallas kernels: none -> 79.9 us  [on_device(): pl.pallas_call(kernel, out_shape=(jax.ShapeDtypeStruct((16, 512), BF16),...]
    dot_general x6 -> x0, matrix products: 11 us -> none  [the longest x1 3.03 us: on_device(): lax.dot_general(both_weights, normed_all, (((2,), (1,)), ((), ())), prefe...]
  transfers between devices with their start and end apart: 5 -> 0, of which waited for: 5 -> 0; matrix products, arithmetic and copies ran while one was open for 1% -> 0% of each run, Pallas kernels for 0% -> 0%
where the time goes in v1:
time: 89.7 us; the launch traced here: 89.4 us
  Pallas kernels  79.9 us (89%)
  local copies, waits for them, and re-layouts  8.82 us (10%)
    pallas_call x1, Pallas kernels, on_device(): pl.pallas_call(kernel, out_shape=(jax.ShapeDtypeStruct((16, 512), BF16),...  79.9 us
    unnamed x18, local copies, waits for them, and re-layouts  8.82 us

profile of v1, /device:TPU:1, one launch (start us, length us, event | category | flops | bytes accessed | tf_op | source)
XLA Modules:
  0.0 89.4 jit_solution(7341660154361124629)
XLA Ops:
  0.6 0.0 copy-start
  0.6 0.9 %copy-done = bf16[160,512]{1,0:T(8,128)(2,1)S(1)} copy-done((bf16[160,512]{1,0:T(8,128)(2,1)S(1)}, bf16[160,512]{1,0:T(8,128)(2,1)}, u32[]{:S(2)}) %copy-start) | copy-done | bytes 163864
  1.6 0.0 copy-start.1
  1.6 0.9 %copy-done.1 = bf16[160,512]{1,0:T(8,128)(2,1)S(1)} copy-done((bf16[160,512]{1,0:T(8,128)(2,1)S(1)}, bf16[160,512]{1,0:T(8,128)(2,1)}, u32[]{:S(2)}) %copy-start.1) | copy-done | bytes 163864
  2.5 0.0 copy-start.2
  2.5 0.9 %copy-done.2 = bf16[160,512]{1,0:T(8,128)(2,1)S(1)} copy-done((bf16[160,512]{1,0:T(8,128)(2,1)S(1)}, bf16[160,512]{1,0:T(8,128)(2,1)}, u32[]{:S(2)}) %copy-start.2) | copy-done | bytes 163864
  3.4 0.0 copy-start.3
  3.4 0.7 copy-done.3
  4.1 0.0 copy-start.4
  4.1 0.7 copy-done.4
  4.8 0.0 copy-start.5
  4.8 0.7 copy-done.5
  5.5 79.9 %shard_map.109 = (bf16[16,512]{1,0:T(8,128)(2,1)S(1)}, bf16[16,512]{1,0:T(8,128)(2,1)S(1)}, f32[160,512]{1,0:T(8,128)S(1)}, f32[160,512]{1,0:T(8,128)S(1)}, f32[...) custom-call(bf16[16,512]{1,0:T(8,128)(2,1)S(1)} %copy-done.3, bf16[16,512]{1,0:T(8,128)(2,1)S(1)} %copy-done.4, ...), custom_call_target="tpu_custom_call" | custom-call | flops 1600000000 | bytes 1600000 | tf_op jit(solution)/shard_map/pallas_call | solution.py:392
  85.4 0.6 copy.18
  86.0 0.6 copy.19
  86.6 0.7 copy.20
  87.3 0.7 copy.21
  88.1 0.7 copy.22
  88.8 0.6 copy.23
Async XLA Ops:
  0.6 0.9 %copy-start = (bf16[160,512]{1,0:T(8,128)(2,1)S(1)}, bf16[160,512]{1,0:T(8,128)(2,1)}, u32[]{:S(2)}) copy-start(bf16[160,512]{1,0:T(8,128)(2,1)} %gate_hbm.1) | copy-start | bytes 491524
  1.6 0.9 %copy-start.1 = (bf16[160,512]{1,0:T(8,128)(2,1)S(1)}, bf16[160,512]{1,0:T(8,128)(2,1)}, u32[]{:S(2)}) copy-start(bf16[160,512]{1,0:T(8,128)(2,1)} %up_hbm.1) | copy-start | bytes 491524
  2.5 0.9 %copy-start.2 = (bf16[160,512]{1,0:T(8,128)(2,1)S(1)}, bf16[160,512]{1,0:T(8,128)(2,1)}, u32[]{:S(2)}) copy-start(bf16[160,512]{1,0:T(8,128)(2,1)} %down_hbm.1) | copy-start | bytes 491524
  3.4 0.7 copy-start.3
  4.1 0.7 copy-start.4
  4.8 0.7 copy-start.5

commit v2 on v1

--- a/solution.py
+++ b/solution.py
@@ -280,36 +280,42 @@
         )
 
     gain_sum = jnp.zeros((1, 512), F32)
+    arrived_b, arrived_g = {}, {}
+
+    def pass_on(step):
+        distance = 5 - step
+        for way in (0, 1):
+            slot = min(2 * distance - 1 + way, 7)
+            there = (ahead, behind)[way]
+            if step > 1 or way == 0:
+                total = branch_part[slot]
+                if (step - 1, way) in arrived_b:
+                    arrived_b[step - 1, way].wait_recv()
+                    total = total + ring_b[step - 2, way].astype(F32)
+                ring_b_out[step - 1, way] = total.astype(BF16)
+                arrived_b[step, way] = remote(
+                    ring_b_out.at[step - 1, way], ring_b.at[step - 1, way], there
+                )
+        for way in (0, 1):
+            slot = min(2 * distance - 1 + way, 7)
+            there = (ahead, behind)[way]
+            if step > 1 or way == 1:
+                total = gn_part[slot]
+                if (step - 1, way) in arrived_g:
+                    arrived_g[step - 1, way].wait_recv()
+                    total = total + ring_g[step - 2, way].astype(F32)
+                ring_g_out[step - 1, way] = rounded(total)
+                arrived_g[step, way] = remote(
+                    ring_g_out.at[step - 1, way], ring_g.at[step - 1, way], there
+                )
+
     gain_sum = terms(4, gain_sum)
-    ring_b_out[0, 0] = branch_part[7].astype(BF16)
-    ring_g_out[0, 1] = rounded(gn_part[7])
-    arrived_b = {0: remote(ring_b_out.at[0, 0], ring_b.at[0, 0], ahead)}
-    arrived_g = {1: remote(ring_g_out.at[0, 1], ring_g.at[0, 1], behind)}
-    for step in (2, 3, 4):
-        distance = 5 - step
-        gain_sum = terms(distance, gain_sum)
-        next_b, next_g = {}, {}
-        for way in (0, 1):
-            slot = 2 * distance - 1 + way
-            there = (ahead, behind)[way]
-            total = branch_part[slot]
-            if way in arrived_b:
-                arrived_b[way].wait_recv()
-                total = total + ring_b[step - 2, way].astype(F32)
-            ring_b_out[step - 1, way] = total.astype(BF16)
-            next_b[way] = remote(ring_b_out.at[step - 1, way], ring_b.at[step - 1, way], there)
-        for way in (0, 1):
-            slot = 2 * distance - 1 + way
-            there = (ahead, behind)[way]
-            total = gn_part[slot]
-            if way in arrived_g:
-                arrived_g[way].wait_recv()
-                total = total + ring_g[step - 2, way].astype(F32)
-            ring_g_out[step - 1, way] = rounded(total)
-            next_g[way] = remote(ring_g_out.at[step - 1, way], ring_g.at[step - 1, way], there)
-        arrived_b, arrived_g = next_b, next_g
-
+    pass_on(1)
     gain_sum = terms(0, gain_sum)
+    gain_sum = terms(1, gain_sum)
+    gain_sum = terms(3, gain_sum)
+    pass_on(2)
+    gain_sum = terms(2, gain_sum)
     dgain[...] = jnp.broadcast_to(gain_sum, (8, 512))
     z_gain = [remote(dgain, dgain_in.at[k - 1], at(dz=k)) for k in range(1, 8)]
 
@@ -321,19 +327,16 @@
         remote(dw.at[pl.ds(3 * UNITS, UNITS)], dw_in.at[1], sibling),
         remote(dd.at[pl.ds(UNITS, UNITS)], dw_in.at[2], sibling),
     ]
-
-    for copy in arrived_b.values():
-        copy.wait_recv()
-    total = branch_part[0] + ring_b[3, 0].astype(F32) + ring_b[3, 1].astype(F32)
-    last_b[...] = total.reshape(4, 16, 512)
-    last_b_out[...] = total.astype(BF16).reshape(4, 16, 512)
-    y_b = [remote(last_b_out.at[piece(k)], last_b_in.at[k - 1], at(dyl=k)) for k in (1, 2, 3)]
-    for copy in arrived_g.values():
-        copy.wait_recv()
-    total = gn_part[0] + ring_g[3, 0].astype(F32) + ring_g[3, 1].astype(F32)
-    last_g[...] = total.reshape(4, 16, 640)
-    last_g_out[...] = rounded(total).reshape(4, 16, 640)
-    y_g = [remote(last_g_out.at[piece(k)], last_g_in.at[k - 1], at(dyl=k)) for k in (1, 2, 3)]
+    pass_on(3)
+
+    for i, (grad, row, out) in enumerate(
+        ((dw, 0, dgate_hbm), (dw, 2 * UNITS, dup_hbm), (dd, 0, ddown_hbm))
+    ):
+        w_sent[i].wait_recv()
+        rows = pl.ds(row, UNITS)
+        grad[rows] = grad[rows] + dw_in[i]
+        bring(grad.at[rows], out)
+    pass_on(4)
 
     for copy in z_gain:
         copy.wait_recv()
@@ -343,11 +346,26 @@
     dgain_y[...] = total
     g_y = [remote(dgain_y, dgain_y_in.at[k - 1], at(dyl=k)) for k in (1, 2, 3)]
 
-    for i, (grad, row, out) in enumerate(((dw, 0, dgate_hbm), (dw, 2 * UNITS, dup_hbm), (dd, 0, ddown_hbm))):
-        w_sent[i].wait_recv()
-        rows = pl.ds(row, UNITS)
-        grad[rows] = grad[rows] + dw_in[i]
-        bring(grad.at[rows], out)
+    arrived_b[4, 0].wait_recv()
+    arrived_b[4, 1].wait_recv()
+    total = branch_part[0] + ring_b[3, 0].astype(F32) + ring_b[3, 1].astype(F32)
+    last_b[...] = total.reshape(4, 16, 512)
+    last_b_out[...] = total.astype(BF16).reshape(4, 16, 512)
+    y_b = [remote(last_b_out.at[piece(k)], last_b_in.at[k - 1], at(dyl=k)) for k in (1, 2, 3)]
+    arrived_g[4, 0].wait_recv()
+    arrived_g[4, 1].wait_recv()
+    total = gn_part[0] + ring_g[3, 0].astype(F32) + ring_g[3, 1].astype(F32)
+    last_g[...] = total.reshape(4, 16, 640)
+    last_g_out[...] = rounded(total).reshape(4, 16, 640)
+    y_g = [remote(last_g_out.at[piece(k)], last_g_in.at[k - 1], at(dyl=k)) for k in (1, 2, 3)]
+
+    for copy in g_y:
+        copy.wait_recv()
+    total = dgain_y[...]
+    for k in range(3):
+        total = total + dgain_y_in[k]
+    dgain_c[...] = total
+    g_c = remote(dgain_c, dgain_c_in, sibling)
 
     for copy in y_b:
         copy.wait_recv()
@@ -357,28 +375,20 @@
     o_branch[...] = total.astype(BF16)
     bring(o_branch, branch_hbm)
 
-    for copy in g_y:
-        copy.wait_recv()
-    total = dgain_y[...]
-    for k in range(3):
-        total = total + dgain_y_in[k]
-    dgain_c[...] = total
-    g_c = remote(dgain_c, dgain_c_in, sibling)
-
+    g_c.wait_recv()
+    o_dgain[...] = (dgain_c[...] + dgain_c_in[...])[0:1]
+    bring(o_dgain, dgain_hbm)
+
+    inv_rms = inverse(hid[0, mine])
+    scaled = own_tok[...].astype(F32) * inv_rms
     for copy in y_g:
         copy.wait_recv()
     total = last_g[mine]
     for k in range(3):
         total = total + last_g_in[k].astype(F32)
     row_mean = (total[:, 512:513] + total[:, 513:514]) / D
-    inv_rms = inverse(hid[0, mine])
-    scaled = own_tok[...].astype(F32) * inv_rms
     o_gtok[...] = (inv_rms * (total[:, 0:512] * gain_v[...] - scaled * row_mean)).astype(BF16)
     bring(o_gtok, gtok_hbm)
-
-    g_c.wait_recv()
-    o_dgain[...] = (dgain_c[...] + dgain_c_in[...])[0:1]
-    bring(o_dgain, dgain_hbm)
 
     for copy in remote.all:
         copy.wait_send()
@@ -386,21 +396,36 @@
         copy.wait()
 
 
+def hand_over(*refs):
+    ins, outs, held = refs[:6], refs[6:12], refs[12:18]
+    in_sem, out_sem = refs[18:]
+    come = [pltpu.make_async_copy(a, b, in_sem.at[i]) for i, (a, b) in enumerate(zip(ins, held))]
+    go = [pltpu.make_async_copy(a, b, out_sem.at[i]) for i, (a, b) in enumerate(zip(held, outs))]
+    for copy in come:
+        copy.start()
+    for one, other in zip(come, go):
+        one.wait()
+        other.start()
+    for copy in go:
+        copy.wait()
+
+
 def on_device(tokens, cotangent, norm_gain, gate_weight, up_weight, down_weight):
     vmem, dma = pltpu.VMEM, pltpu.SemaphoreType.DMA
     grad = jax.ShapeDtypeStruct((UNITS, 512), F32)
+    shapes = (
+        jax.ShapeDtypeStruct((16, 512), BF16),
+        jax.ShapeDtypeStruct((16, 512), BF16),
+        grad,
+        grad,
+        grad,
+        jax.ShapeDtypeStruct((1, 512), F32),
+    )
     outs = pl.pallas_call(
         kernel,
-        out_shape=(
-            jax.ShapeDtypeStruct((16, 512), BF16),
-            jax.ShapeDtypeStruct((16, 512), BF16),
-            grad,
-            grad,
-            grad,
-            jax.ShapeDtypeStruct((1, 512), F32),
-        ),
-        in_specs=[pl.BlockSpec(memory_space=pl.ANY)] * 6,
-        out_specs=[pl.BlockSpec(memory_space=pl.ANY)] * 6,
+        out_shape=shapes,
+        in_specs=[pl.BlockSpec(memory_space=pltpu.HBM)] * 6,
+        out_specs=[pl.BlockSpec(memory_space=pltpu.HBM)] * 6,
         scratch_shapes=[
             vmem((16, 512), BF16),
             vmem((1, 512), F32),
@@ -446,10 +471,18 @@
             dma((16,)),
         ],
         compiler_params=pltpu.CompilerParams(
-            collective_id=0, has_side_effects=True, vmem_limit_bytes=48 * 1024 * 1024
+            collective_id=0, has_side_effects=True, vmem_limit_bytes=63 * 1024 * 1024
         ),
         cost_estimate=pl.CostEstimate(flops=1_600_000_000, bytes_accessed=1_600_000, transcendentals=50_000),
     )(tokens, cotangent, norm_gain.reshape(1, 512), gate_weight, up_weight, down_weight)
+    outs = pl.pallas_call(
+        hand_over,
+        out_shape=shapes,
+        in_specs=[pl.BlockSpec(memory_space=pltpu.HBM)] * 6,
+        out_specs=[pl.BlockSpec(memory_space=pltpu.HBM)] * 6,
+        scratch_shapes=[*(vmem(a.shape, a.dtype) for a in shapes), dma((6,)), dma((6,))],
+        compiler_params=pltpu.CompilerParams(vmem_limit_bytes=63 * 1024 * 1024),
+    )(*outs)
     return (*outs[:5], outs[5].reshape(512))
 
 

time: 89.7 us -> 77.9 us (0.87); the launches traced: 89.4 us -> 76.4 us
  local copies, waits for them, and re-layouts: 8.82 us -> 0 us
  Pallas kernels: 79.9 us -> 75.8 us
    unnamed x18 -> x0, local copies, waits for them, and re-layouts: 8.82 us -> none
    pallas_call x1 -> x2, Pallas kernels: 79.9 us -> 75.8 us  [the longest x1 73.7 us: on_device(): pl.pallas_call(kernel, out_shape=shapes, in_specs=[pl.BlockSpec(memory_sp...]
where the time goes in v2:
time: 77.9 us; the launch traced here: 76.4 us
  Pallas kernels  75.8 us (97%)
    pallas_call x1, Pallas kernels, on_device(): pl.pallas_call(kernel, out_shape=shapes, in_specs=[pl.BlockSpec(memory_sp...  73.7 us
    pallas_call x1, Pallas kernels, on_device(): pl.pallas_call(hand_over, out_shape=shapes, in_specs=[pl.BlockSpec(memory...  2.05 us

profile of v2, /device:TPU:1, one launch (start us, length us, event | category | flops | bytes accessed | tf_op | source)
XLA Modules:
  0.0 76.4 jit_solution(12902256386225582207)
XLA Ops:
  0.6 73.7 %shard_map.109 = (bf16[16,512]{1,0:T(8,128)(2,1)}, bf16[16,512]{1,0:T(8,128)(2,1)}, f32[160,512]{1,0:T(8,128)}, f32[160,512]{1,0:T(8,128)}, f32[160,512]{1,0:T(8,128)}, /*index=5*/f32[1,512]{1,0:T(1,128)}) custom-call(bf16[16,512]{1,0:T(8,128)(2,1)} %tok_hbm.1, bf16[16,512]{1,0:T(8,128)(2,1)} %cot_hbm.1, f32[1,512]{1,0:T(1,128)} %bitcast.2, ...), custom_call_target="tpu_custom_call" | custom-call | flops 1600000000 | bytes 1600000 | tf_op jit(solution)/shard_map/pallas_call | solution.py:424
  74.4 2.1 %shard_map.110 = (bf16[16,512]{1,0:T(8,128)(2,1)}, bf16[16,512]{1,0:T(8,128)(2,1)}, f32[160,512]{1,0:T(8,128)}, f32[160,512]{1,0:T(8,128)}, f32[160,512]{1,0:T(8,128)}, /*index=5*/f32[1,512]{1,0:T(1,128)}) custom-call(bf16[16,512]{1,0:T(8,128)(2,1)} %get-tuple-element.18.refs_0_, bf16[16,512]{1,0:T(8,128)(2,1)} %get-tuple-element.19.refs_1_, ...), custom_call_target="tpu_custom_call" | custom-call | tf_op jit(solution)/shard_map/pallas_call | solution.py:478

commit v3 on v2

--- a/solution.py
+++ b/solution.py
@@ -69,14 +69,14 @@
         return copy
 
 
-N_COPIES = 120
+N_COPIES = 128
 
 
 def kernel(
     tok_hbm, cot_hbm, gain_hbm, gate_hbm, up_hbm, down_hbm,
     branch_hbm, gtok_hbm, dgate_hbm, dup_hbm, ddown_hbm, dgain_hbm,
     own_tok, gain_v, tok, cot, w, w_high, w_low, wd, part, part_own, rx, y_out, y_in, hid,
-    normed, branch_part, gn_part, ring_b, ring_g, ring_b_out, ring_g_out,
+    normed, branch_part, gn_part, sums_in, sums_out,
     last_b, last_g, last_b_out, last_g_out, last_b_in, last_g_in,
     dw, dd, dw_in, dgain, dgain_in, dgain_y, dgain_y_in, dgain_c, dgain_c_in,
     o_branch, o_gtok, o_dgain,
@@ -95,6 +95,14 @@
     sibling, across = at(dc=1), at(dyh=1)
     ahead, behind = at(dz=1), at(dz=7)
 
+    barrier = pltpu.get_barrier_semaphore()
+    partners = [across, *(at(dz=k) for k in (4, 3, 5, 2, 6, 1, 7))]
+    partners += [at(dyl=k) for k in (3, 2, 1)]
+    partners += [at(dx=k) for k in (2, 1, 3)]
+    partners += [sibling]
+    for device in partners:
+        pl.semaphore_signal(barrier, 1, device_id=device, device_id_type=MESH)
+
     def piece(k):
         return lax.rem(k - x + 8, 4)
 
@@ -115,13 +123,6 @@
     b_up = bring(up_hbm, w.at[pl.ds(2 * UNITS, UNITS)])
     b_down = bring(down_hbm, wd.at[pl.ds(0, UNITS)])
 
-    barrier = pltpu.get_barrier_semaphore()
-    partners = [sibling, across]
-    partners += [at(dx=k) for k in (1, 2, 3)]
-    partners += [at(dyl=k) for k in (1, 2, 3)]
-    partners += [at(dz=k) for k in range(1, 8)]
-    for device in partners:
-        pl.semaphore_signal(barrier, 1, device_id=device, device_id_type=MESH)
     wd[pl.ds(2 * UNITS, 64)] = jnp.zeros((64, 512), BF16)
     pl.semaphore_wait(barrier, len(partners))
 
@@ -149,22 +150,28 @@
     b_down.wait()
     b_own.wait()
 
-    def ring(buffer, step, both, way):
+    def ring(buffer, step, way, arrived):
         copies = []
-        if both or way > 0:
-            src = 0 if step == 1 else 2 * (step - 1)
-            copies.append(remote(buffer.at[src], buffer.at[min(2 * step, 7)], ahead))
-        if both or way < 0:
-            src = 0 if step == 1 else 2 * (step - 1) - 1
-            copies.append(remote(buffer.at[src], buffer.at[2 * step - 1], behind))
+        for half in (0, 1):
+            rows = pl.ds(2 * half, 2)
+            for copy in arrived[half * len(arrived) // 2 : (half + 1) * len(arrived) // 2]:
+                copy.wait_recv()
+            if step < 5 and (step < 4 or way > 0):
+                src = 0 if step == 1 else 2 * (step - 1)
+                dst = min(2 * step, 7)
+                copies.append(remote(buffer.at[src, rows], buffer.at[dst, rows], ahead))
+            if step < 5 and (step < 4 or way < 0):
+                src = 0 if step == 1 else 2 * (step - 1) - 1
+                dst = 2 * step - 1
+                copies.append(remote(buffer.at[src, rows], buffer.at[dst, rows], behind))
         return copies
 
     for copy in y_tok:
         copy.wait_recv()
-    r_tok = ring(tok, 1, True, 0)
+    r_tok = ring(tok, 1, -1, [])
     for copy in y_cot:
         copy.wait_recv()
-    r_cot = ring(cot, 1, True, 0)
+    r_cot = ring(cot, 1, 1, [])
 
     s_gate.wait_recv()
     fold(1)
@@ -210,17 +217,12 @@
     x_sent, y_sent = [], []
     x_sent.append(multiply(0))
     for step in (1, 2, 3, 4):
-        for copy in r_tok:
-            copy.wait_recv()
-        if step < 4:
-            r_tok = ring(tok, step + 1, step < 3, -1)
-        for copy in r_cot:
-            copy.wait_recv()
-        if step < 4:
-            r_cot = ring(cot, step + 1, step < 3, 1)
+        r_tok = ring(tok, step + 1, -1, r_tok)
+        r_cot = ring(cot, step + 1, 1, r_cot)
         x_sent.append(multiply(step))
-        y_sent.append(add_x(step - 1, x_sent[step - 1]))
-    y_sent.append(add_x(4, x_sent[4]))
+        if step > 1:
+            y_sent.append(add_x(step - 2, x_sent[step - 2]))
+    y_sent.append(add_x(3, x_sent[3]))
 
     def pointwise(g):
         a, b = GROUPS[g]
@@ -250,12 +252,15 @@
             for k in (1, 2, 3)
         ]
 
-    h_sent = {g: pointwise(g) for g in (0, 1, 4, 3, 2)}
+    h_sent = {0: pointwise(0)}
+    y_sent.append(add_x(4, x_sent[4]))
+    for g in (1, 4, 3, 2):
+        h_sent[g] = pointwise(g)
 
     def inverse(block):
         return block[:, 962:963].astype(F32) + block[:, 963:964].astype(F32)
 
-    def terms(g, gain_sum):
+    def terms(g, sums):
         a, b = GROUPS[g]
         n = b - a
         for copy in h_sent[g]:
@@ -265,58 +270,56 @@
         grad = dot(block[:, 0:640], w[...])
         scaled = tok[a:b].reshape(n * 64, 512).astype(F32) * inverse(block)
         normed[a:b] = (scaled * gain_v[...]).astype(BF16).reshape(n, 64, 512)
-        gain_sum = gain_sum + jnp.sum(grad * scaled, axis=0, keepdims=True)
-        gn_part[a:b, :, 0:512] = grad.reshape(n, 64, 512)
+        gn_part[a:b] = grad.reshape(n, 64, 512)
         along = block[:, 960:961].astype(F32) + block[:, 961:962].astype(F32)
-        extra = put(jnp.zeros((n * 64, 128), F32), 0, along)
-        gn_part[a:b, :, 512:640] = extra.reshape(n, 64, 128)
-        return gain_sum
-
-    def rounded(total):
-        along = total[:, 512:513] + total[:, 513:514]
-        return jnp.concatenate(
-            [total[:, 0:512].astype(BF16), put(total[:, 512:640], 0, *pair(along)).astype(BF16)],
-            axis=1,
+        row = lax.broadcasted_iota(jnp.int32, (n * 64, 512), 0)
+        lane = lax.broadcasted_iota(jnp.int32, (n * 64, 512), 1)
+        along = jnp.where(lane == row + a * 64, along, 0.0)
+        return (
+            sums[0] + jnp.sum(grad * scaled, axis=0, keepdims=True),
+            sums[1] + jnp.sum(along, axis=0, keepdims=True),
         )
 
-    gain_sum = jnp.zeros((1, 512), F32)
-    arrived_b, arrived_g = {}, {}
+    def eight_rows(ref, first, second):
+        for i in range(4):
+            lanes = slice(i * 128, (i + 1) * 128)
+            ref[i : i + 1] = first[:, lanes]
+            ref[4 + i : 5 + i] = second[:, lanes]
+
+    sums = (jnp.zeros((1, 512), F32), jnp.zeros((1, 512), F32))
+    streams = [(branch_part, 0), (branch_part, 1), (gn_part, 0), (gn_part, 1)]
+    arrived = {}
+
+    def so_far(slot, stream, *known):
+        source, half = streams[stream]
+        total = source[slot, :, half * 256 : (half + 1) * 256]
+        for step, way in known:
+            if (step, way, stream) in arrived:
+                arrived[step, way, stream].wait_recv()
+                total = total + sums_in[step - 1, way, stream].astype(F32)
+        return total
 
     def pass_on(step):
-        distance = 5 - step
-        for way in (0, 1):
-            slot = min(2 * distance - 1 + way, 7)
-            there = (ahead, behind)[way]
-            if step > 1 or way == 0:
-                total = branch_part[slot]
-                if (step - 1, way) in arrived_b:
-                    arrived_b[step - 1, way].wait_recv()
-                    total = total + ring_b[step - 2, way].astype(F32)
-                ring_b_out[step - 1, way] = total.astype(BF16)
-                arrived_b[step, way] = remote(
-                    ring_b_out.at[step - 1, way], ring_b.at[step - 1, way], there
+        for stream in range(4):
+            for way in (0, 1):
+                if step == 1 and way != stream // 2:
+                    continue
+                slot = min(2 * (5 - step) - 1 + way, 7)
+                sums_out[step - 1, way, stream] = so_far(slot, stream, (step - 1, way)).astype(BF16)
+                arrived[step, way, stream] = remote(
+                    sums_out.at[step - 1, way, stream],
+                    sums_in.at[step - 1, way, stream],
+                    (ahead, behind)[way],
                 )
-        for way in (0, 1):
-            slot = min(2 * distance - 1 + way, 7)
-            there = (ahead, behind)[way]
-            if step > 1 or way == 1:
-                total = gn_part[slot]
-                if (step - 1, way) in arrived_g:
-                    arrived_g[step - 1, way].wait_recv()
-                    total = total + ring_g[step - 2, way].astype(F32)
-                ring_g_out[step - 1, way] = rounded(total)
-                arrived_g[step, way] = remote(
-                    ring_g_out.at[step - 1, way], ring_g.at[step - 1, way], there
-                )
-
-    gain_sum = terms(4, gain_sum)
+
+    sums = terms(4, sums)
     pass_on(1)
-    gain_sum = terms(0, gain_sum)
-    gain_sum = terms(1, gain_sum)
-    gain_sum = terms(3, gain_sum)
+    sums = terms(0, sums)
+    sums = terms(1, sums)
+    sums = terms(3, sums)
     pass_on(2)
-    gain_sum = terms(2, gain_sum)
-    dgain[...] = jnp.broadcast_to(gain_sum, (8, 512))
+    sums = terms(2, sums)
+    eight_rows(dgain, *sums)
     z_gain = [remote(dgain, dgain_in.at[k - 1], at(dz=k)) for k in range(1, 8)]
 
     every = hid[...].reshape(512, 1024)
@@ -340,24 +343,27 @@
 
     for copy in z_gain:
         copy.wait_recv()
-    total = dgain[...]
-    for k in range(7):
-        total = total + dgain_in[k]
-    dgain_y[...] = total
+    gain_total, along = dgain[0:4], dgain[4:5]
+    low = lax.broadcasted_iota(jnp.int32, (1, 128), 1) < 64
+    for k in range(1, 8):
+        slot = 2 * k - 1 if k < 5 else 2 * (8 - k)
+        gain_total = gain_total + dgain_in[k - 1, 0:4]
+        row = dgain_in[k - 1, 4 + slot // 2 : 5 + slot // 2]
+        along = along + (pltpu.roll(row, 64, 1) if slot % 2 else row)
+    dgain_y[0:4] = gain_total
+    dgain_y[4:8] = jnp.broadcast_to(jnp.where(low, along, 0.0), (4, 128))
     g_y = [remote(dgain_y, dgain_y_in.at[k - 1], at(dyl=k)) for k in (1, 2, 3)]
 
-    arrived_b[4, 0].wait_recv()
-    arrived_b[4, 1].wait_recv()
-    total = branch_part[0] + ring_b[3, 0].astype(F32) + ring_b[3, 1].astype(F32)
-    last_b[...] = total.reshape(4, 16, 512)
-    last_b_out[...] = total.astype(BF16).reshape(4, 16, 512)
-    y_b = [remote(last_b_out.at[piece(k)], last_b_in.at[k - 1], at(dyl=k)) for k in (1, 2, 3)]
-    arrived_g[4, 0].wait_recv()
-    arrived_g[4, 1].wait_recv()
-    total = gn_part[0] + ring_g[3, 0].astype(F32) + ring_g[3, 1].astype(F32)
-    last_g[...] = total.reshape(4, 16, 640)
-    last_g_out[...] = rounded(total).reshape(4, 16, 640)
-    y_g = [remote(last_g_out.at[piece(k)], last_g_in.at[k - 1], at(dyl=k)) for k in (1, 2, 3)]
+    def finish(array, total, out, landing):
+        for half in (0, 1):
+            lanes = slice(half * 256, (half + 1) * 256)
+            part_sum = so_far(0, 2 * array + half, (4, 0), (4, 1)).reshape(4, 16, 256)
+            total[:, :, lanes] = part_sum
+            out[:, :, lanes] = part_sum.astype(BF16)
+        return [remote(out.at[piece(k)], landing.at[k - 1], at(dyl=k)) for k in (1, 2, 3)]
+
+    y_b = finish(0, last_b, last_b_out, last_b_in)
+    y_g = finish(1, last_g, last_g_out, last_g_in)
 
     for copy in g_y:
         copy.wait_recv()
@@ -365,6 +371,12 @@
     for k in range(3):
         total = total + dgain_y_in[k]
     dgain_c[...] = total
+    row = lax.broadcasted_iota(jnp.int32, (16, 128), 0)
+    lane = lax.broadcasted_iota(jnp.int32, (16, 128), 1)
+    along = jnp.where(lane == row + mine * 16, dgain_y[4:5], 0.0)
+    for k in (1, 2, 3):
+        along = along + jnp.where(lane == row + piece(k) * 16, dgain_y_in[k - 1, 4:5], 0.0)
+    row_mean = jnp.sum(along, axis=1, keepdims=True) / D
     g_c = remote(dgain_c, dgain_c_in, sibling)
 
     for copy in y_b:
@@ -376,7 +388,7 @@
     bring(o_branch, branch_hbm)
 
     g_c.wait_recv()
-    o_dgain[...] = (dgain_c[...] + dgain_c_in[...])[0:1]
+    o_dgain[...] = (dgain_c[...] + dgain_c_in[...])[0:4]
     bring(o_dgain, dgain_hbm)
 
     inv_rms = inverse(hid[0, mine])
@@ -386,8 +398,7 @@
     total = last_g[mine]
     for k in range(3):
         total = total + last_g_in[k].astype(F32)
-    row_mean = (total[:, 512:513] + total[:, 513:514]) / D
-    o_gtok[...] = (inv_rms * (total[:, 0:512] * gain_v[...] - scaled * row_mean)).astype(BF16)
+    o_gtok[...] = (inv_rms * (total * gain_v[...] - scaled * row_mean)).astype(BF16)
     bring(o_gtok, gtok_hbm)
 
     for copy in remote.all:
@@ -419,7 +430,7 @@
         grad,
         grad,
         grad,
-        jax.ShapeDtypeStruct((1, 512), F32),
+        jax.ShapeDtypeStruct((4, 128), F32),
     )
     outs = pl.pallas_call(
         kernel,
@@ -443,29 +454,27 @@
             vmem((8, 4, 16, 1024), BF16),
             vmem((8, 64, 512), BF16),
             vmem((8, 64, 512), F32),
-            vmem((8, 64, 640), F32),
-            vmem((4, 2, 64, 512), BF16),
-            vmem((4, 2, 64, 640), BF16),
-            vmem((4, 2, 64, 512), BF16),
-            vmem((4, 2, 64, 640), BF16),
+            vmem((8, 64, 512), F32),
+            vmem((4, 2, 4, 64, 256), BF16),
+            vmem((4, 2, 4, 64, 256), BF16),
             vmem((4, 16, 512), F32),
-            vmem((4, 16, 640), F32),
+            vmem((4, 16, 512), F32),
             vmem((4, 16, 512), BF16),
-            vmem((4, 16, 640), BF16),
+            vmem((4, 16, 512), BF16),
             vmem((3, 16, 512), BF16),
-            vmem((3, 16, 640), BF16),
+            vmem((3, 16, 512), BF16),
             vmem((4 * UNITS, 512), F32),
             vmem((384, 512), F32),
             vmem((3, UNITS, 512), F32),
-            vmem((8, 512), F32),
-            vmem((7, 8, 512), F32),
-            vmem((8, 512), F32),
-            vmem((3, 8, 512), F32),
-            vmem((8, 512), F32),
-            vmem((8, 512), F32),
+            vmem((8, 128), F32),
+            vmem((7, 8, 128), F32),
+            vmem((8, 128), F32),
+            vmem((3, 8, 128), F32),
+            vmem((8, 128), F32),
+            vmem((8, 128), F32),
             vmem((16, 512), BF16),
             vmem((16, 512), BF16),
-            vmem((1, 512), F32),
+            vmem((4, 128), F32),
             dma((N_COPIES,)),
             dma((N_COPIES,)),
             dma((16,)),

time: 77.9 us -> 73.8 us (0.947)
  Pallas kernels: 75.8 us -> 72.4 us
    pallas_call x1, Pallas kernels: 73.7 us -> 70.4 us  [on_device(): pl.pallas_call(kernel, out_shape=shapes, in_specs=[pl.BlockSpec(memory_sp...]
where the time goes in v3:
time: 73.8 us; the launch traced here: 73.1 us
  Pallas kernels  72.4 us (98%)
    pallas_call x1, Pallas kernels, on_device(): pl.pallas_call(kernel, out_shape=shapes, in_specs=[pl.BlockSpec(memory_sp...  70.4 us
    pallas_call x1, Pallas kernels, on_device(): pl.pallas_call(hand_over, out_shape=shapes, in_specs=[pl.BlockSpec(memory...  2.05 us

profile of v3, /device:TPU:1, one launch (start us, length us, event | category | flops | bytes accessed | tf_op | source)
XLA Modules:
  0.0 73.1 jit_solution(2656835878156503768)
XLA Ops:
  0.6 70.4 %shard_map.109 = (bf16[16,512]{1,0:T(8,128)(2,1)}, bf16[16,512]{1,0:T(8,128)(2,1)}, f32[160,512]{1,0:T(8,128)}, f32[160,512]{1,0:T(8,128)}, f32[160,512]{1,0:T(8,128)}, /*index=5*/f32[4,128]{1,0:T(4,128)}) custom-call(bf16[16,512]{1,0:T(8,128)(2,1)} %tok_hbm.1, bf16[16,512]{1,0:T(8,128)(2,1)} %cot_hbm.1, f32[1,512]{1,0:T(1,128)} %bitcast.2, ...), custom_call_target="tpu_custom_call" | custom-call | flops 1600000000 | bytes 1600000 | tf_op jit(solution)/shard_map/pallas_call | solution.py:435
  71.0 2.1 %shard_map.110 = (bf16[16,512]{1,0:T(8,128)(2,1)}, bf16[16,512]{1,0:T(8,128)(2,1)}, f32[160,512]{1,0:T(8,128)}, f32[160,512]{1,0:T(8,128)}, f32[160,512]{1,0:T(8,128)}, /*index=5*/f32[4,128]{1,0:T(4,128)}) custom-call(bf16[16,512]{1,0:T(8,128)(2,1)} %get-tuple-element.18.refs_0_, bf16[16,512]{1,0:T(8,128)(2,1)} %get-tuple-element.19.refs_1_, ...), custom_call_target="tpu_custom_call" | custom-call | tf_op jit(solution)/shard_map/pallas_call | solution.py:487

commit v4 on v3

--- a/solution.py
+++ b/solution.py
@@ -408,16 +408,11 @@
 
 
 def hand_over(*refs):
-    ins, outs, held = refs[:6], refs[6:12], refs[12:18]
-    in_sem, out_sem = refs[18:]
-    come = [pltpu.make_async_copy(a, b, in_sem.at[i]) for i, (a, b) in enumerate(zip(ins, held))]
-    go = [pltpu.make_async_copy(a, b, out_sem.at[i]) for i, (a, b) in enumerate(zip(held, outs))]
-    for copy in come:
+    ins, outs, sem = refs[:6], refs[6:12], refs[12]
+    copies = [pltpu.make_async_copy(a, b, sem.at[i]) for i, (a, b) in enumerate(zip(ins, outs))]
+    for copy in copies:
         copy.start()
-    for one, other in zip(come, go):
-        one.wait()
-        other.start()
-    for copy in go:
+    for copy in copies:
         copy.wait()
 
 
@@ -434,9 +429,9 @@
     )
     outs = pl.pallas_call(
         kernel,
-        out_shape=shapes,
+        out_shape=tuple(vmem(a.shape, a.dtype) for a in shapes),
         in_specs=[pl.BlockSpec(memory_space=pltpu.HBM)] * 6,
-        out_specs=[pl.BlockSpec(memory_space=pltpu.HBM)] * 6,
+        out_specs=[pl.BlockSpec(memory_space=pl.ANY)] * 6,
         scratch_shapes=[
             vmem((16, 512), BF16),
             vmem((1, 512), F32),
@@ -480,17 +475,17 @@
             dma((16,)),
         ],
         compiler_params=pltpu.CompilerParams(
-            collective_id=0, has_side_effects=True, vmem_limit_bytes=63 * 1024 * 1024
+            collective_id=0, has_side_effects=True, vmem_limit_bytes=60 * 1024 * 1024
         ),
         cost_estimate=pl.CostEstimate(flops=1_600_000_000, bytes_accessed=1_600_000, transcendentals=50_000),
     )(tokens, cotangent, norm_gain.reshape(1, 512), gate_weight, up_weight, down_weight)
     outs = pl.pallas_call(
         hand_over,
         out_shape=shapes,
-        in_specs=[pl.BlockSpec(memory_space=pltpu.HBM)] * 6,
+        in_specs=[pl.BlockSpec(memory_space=pl.ANY)] * 6,
         out_specs=[pl.BlockSpec(memory_space=pltpu.HBM)] * 6,
-        scratch_shapes=[*(vmem(a.shape, a.dtype) for a in shapes), dma((6,)), dma((6,))],
-        compiler_params=pltpu.CompilerParams(vmem_limit_bytes=63 * 1024 * 1024),
+        scratch_shapes=[dma((6,))],
+        compiler_params=pltpu.CompilerParams(vmem_limit_bytes=2 * 1024 * 1024),
     )(*outs)
     return (*outs[:5], outs[5].reshape(512))
 

time: 73.8 us -> 72.4 us (0.981)
  Pallas kernels: 72.4 us -> 71.1 us
    pallas_call x1, Pallas kernels: 2.05 us -> 1.01 us  [on_device(): pl.pallas_call(hand_over, out_shape=shapes, in_specs=[pl.BlockSpec(memory...]
where the time goes in v4:
time: 72.4 us; the launch traced here: 71.8 us
  Pallas kernels  71.1 us (98%)
    pallas_call x1, Pallas kernels, on_device(): pl.pallas_call(kernel, out_shape=tuple((vmem(a.shape, a.dtype) for a in s...  70.1 us

profile of v4, /device:TPU:1, one launch (start us, length us, event | category | flops | bytes accessed | tf_op | source)
XLA Modules:
  0.0 71.8 jit_solution(10133096981376073113)
XLA Ops:
  0.6 70.1 %shard_map.109 = (bf16[16,512]{1,0:T(8,128)(2,1)S(1)}, bf16[16,512]{1,0:T(8,128)(2,1)S(1)}, f32[160,512]{1,0:T(8,128)S(1)}, f32[160,512]{1,0:T(8,128)S(1)}, f32[...) custom-call(bf16[16,512]{1,0:T(8,128)(2,1)} %tok_hbm.1, bf16[16,512]{1,0:T(8,128)(2,1)} %cot_hbm.1, f32[1,512]{1,0:T(1,128)} %bitcast.2, ...), custom_call_target="tpu_custom_call" | custom-call | flops 1600000000 | bytes 1600000 | tf_op jit(solution)/shard_map/pallas_call | solution.py:430
  70.8 1.0 %shard_map.110 = (bf16[16,512]{1,0:T(8,128)(2,1)}, bf16[16,512]{1,0:T(8,128)(2,1)}, f32[160,512]{1,0:T(8,128)}, f32[160,512]{1,0:T(8,128)}, f32[160,512]{1,0:T(8,128)}, /*index=5*/f32[4,128]{1,0:T(4,128)}) custom-call(bf16[16,512]{1,0:T(8,128)(2,1)S(1)} %get-tuple-element.18.refs_0_, bf16[16,512]{1,0:T(8,128)(2,1)S(1)} %get-tuple-element.19.refs_1_, ...), custom_call_target="tpu_custom_call" | custom-call | tf_op jit(solution)/shard_map/pallas_call | solution.py:482
